TPU v7x, 32 devices: a whole 2x2x4 slice. The times are simulated.
32 devices in a mesh: row: 8 (over y, x, core), col: 4 (over z).
Axes of the slice: x: 2, y: 2, z: 4, core: 2. Of those that a mesh axis runs over, the one named last changes fastest.
Arguments:
- features: float32 [8192, 256], P(('row', 'col')), may hold values from -6 to 6
- loader_perm: int32 [8192], P(('row', 'col')), may hold values from 0 to 8191, as said below
- block_values: float32 [8, 4, 256, 4096], P('row', 'col'), may hold values from -0.09375 to 0.09375
- block_row: int32 [8, 4, 256], P('row', 'col'), may hold values from 0 to 31
- block_column: int32 [8, 4, 256], P('row', 'col'), may hold values from 0 to 15
- tile_count: int32 [8, 4], P('row', 'col'), may hold values from 32 to 256, as said below
- weight: float32 [256, 256], replicated, may hold values from -0.375 to 0.375
- bias_vector: float32 [256], replicated, may hold values from -0.5 to 0.5
- cotangent: float32 [8192, 256], P(('row', 'col')), may hold values from -6 to 6
Outputs:
- output: float32 [8192, 256], P(('row', 'col'))
- grad_x: float32 [8192, 256], P(('row', 'col'))
- grad_w: float32 [256, 256], replicated
- grad_b: float32 [256], replicated
Inputs may be any that keep to these rules, and one draw needn't show every extreme that they name: `loader_perm`: every grid position appears once; the 256 loader rows of any one device name the same number of positions, 256 divided by the number of devices, in each aligned block of 256 grid positions. `tile_count`: every count is 256 divided by 1, 2, 4 or 8; a block position may appear in several slots of a tile, and such blocks add.
All inputs are finite; a program needn't handle non-finite values.
Results may differ from a plain program's by a relative error of at most 0.0003.
Values sent between devices are 32-bit elements; how exact they have to be, the bound alone decides.
A program may use at most 128 MiB of HBM per device.

v0:
```python
import math

import jax
import jax.numpy as jnp
from jax import lax
from jax.sharding import PartitionSpec as P

precise = lax.Precision.HIGHEST


def accumulate(
    accumulated,
    source_blocks,
    tile_vals,
    source_at,
    target_at,
    live_count,
    pattern,
    group_size,
    group_turns,
    block_size,
):

    def one_group(turn, partial_sum):
        first_slot = turn * group_size
        group_vals = lax.dynamic_slice_in_dim(tile_vals, first_slot, group_size, 0)
        from_at = lax.dynamic_slice_in_dim(source_at, first_slot, group_size, 0)
        into_at = lax.dynamic_slice_in_dim(target_at, first_slot, group_size, 0)
        alive = first_slot + jnp.arange(group_size, dtype=jnp.int32) < live_count
        group_vals = jnp.where(alive[:, None], group_vals, jnp.zeros_like(group_vals))
        group_vals = group_vals.reshape(group_size, block_size, block_size)
        terms = jnp.einsum(pattern, group_vals, source_blocks[from_at], precision=precise)
        return partial_sum.at[into_at].add(terms)

    return lax.fori_loop(0, group_turns, one_group, accumulated)


def on_device(
    features,
    loader_perm,
    block_values,
    block_row,
    block_column,
    tile_count,
    weight,
    bias_vector,
    cotangent,
):
    node_dev, feat_width = features.shape
    row_devices = lax.axis_size("row")
    col_devices = lax.axis_size("col")
    devices = row_devices * col_devices
    row_index = lax.axis_index("row")
    group_rows = col_devices * node_dev
    tile_vals = block_values[0, 0]
    tile_rows = block_row[0, 0]
    tile_columns = block_column[0, 0]
    live_count = tile_count[0, 0]
    block_size = math.isqrt(tile_vals.shape[-1])
    slot_total = tile_vals.shape[0]
    group_size = math.gcd(slot_total, 128)
    group_turns = slot_total // group_size
    per_group = node_dev // row_devices
    ordering = jnp.argsort(loader_perm // group_rows, stable=True)
    sent_rows = jnp.broadcast_to(
        features[ordering].reshape(row_devices, 1, per_group, feat_width),
        (row_devices, col_devices, per_group, feat_width),
    ).reshape(devices, per_group, feat_width)
    sent_ids = jnp.broadcast_to(
        loader_perm[ordering].astype(jnp.float32).reshape(row_devices, 1, per_group),
        (row_devices, col_devices, per_group),
    ).reshape(devices, per_group)
    got_rows, got_ids = (
        lax.all_to_all(sent_rows, ("row", "col"), split_axis=0, concat_axis=0, tiled=True),
        lax.all_to_all(sent_ids, ("row", "col"), split_axis=0, concat_axis=0, tiled=True),
    )
    local_pos = got_ids.reshape(group_rows).astype(jnp.int32) - row_index * group_rows
    panel_rows = got_rows.reshape(group_rows, feat_width)[jnp.argsort(local_pos)]
    out_blocks = row_devices * node_dev // block_size
    in_blocks = group_rows // block_size
    partial_value = accumulate(
        jnp.zeros((out_blocks, block_size, feat_width), jnp.float32),
        panel_rows.reshape(in_blocks, block_size, feat_width),
        tile_vals,
        tile_columns,
        tile_rows,
        live_count,
        "kab,kbf->kaf",
        group_size,
        group_turns,
        block_size,
    )
    partial_value = partial_value.reshape(row_devices * node_dev, feat_width)
    hidden = lax.psum_scatter(partial_value, "row", scatter_dimension=0, tiled=True)
    preact = jnp.dot(hidden, weight, precision=precise) + bias_vector
    squashed = jax.nn.sigmoid(preact)
    output = preact * squashed
    grad_pre = cotangent * squashed * (1.0 + preact * (1.0 - squashed))
    grad_hidden = jnp.dot(grad_pre, weight.T, precision=precise)
    column = lax.all_gather(grad_hidden, "row", axis=0, tiled=True)
    partial_x = accumulate(
        jnp.zeros((in_blocks, block_size, feat_width), jnp.float32),
        column.reshape(out_blocks, block_size, feat_width),
        tile_vals,
        tile_rows,
        tile_columns,
        live_count,
        "kba,kbf->kaf",
        group_size,
        group_turns,
        block_size,
    )
    grad_x = lax.psum_scatter(
        partial_x.reshape(group_rows, feat_width), "col", scatter_dimension=0, tiled=True
    )
    local_w = jnp.einsum("nf,ng->fg", hidden, grad_pre, precision=precise)
    local_b = jnp.sum(grad_pre, axis=0)
    grad_w, grad_b = lax.psum((local_w, local_b), ("row", "col"))
    norm_scale = 1.0 / math.sqrt(node_dev * devices)
    return (output, grad_x, grad_w * norm_scale, grad_b * norm_scale)


def solution(mesh):
    in_specs = (
        P(("row", "col"), None),
        P(("row", "col")),
        P("row", "col", None, None),
        P("row", "col", None),
        P("row", "col", None),
        P("row", "col"),
        P(),
        P(),
        P(("row", "col"), None),
    )
    out_specs = (P(("row", "col"), None), P(("row", "col"), None), P(), P())
    return jax.shard_map(
        on_device, mesh=mesh, in_specs=in_specs, out_specs=out_specs, check_vma=False
    )
```

profile of v0, /device:TPU:27, one launch (start us, length us, event | category | flops | bytes accessed | tf_op | source)
XLA Modules:
  0.0 390.6 jit_solution(15035415348022640324)
XLA Ops:
  7.9 3.2 sort.34
  13.8 6.2 %all-to-all-start.1 = ((f32[32,1,32]{2,1,0:T(1,128)}), f32[32,1,32]{2,1,0:T(1,128)S(1)}, u32[]{:S(2)}, u32[]{:S(2)}) async-start(f32[32,1,32]{2,1,0:T(1,128)} %bitcast.9), calls=%async_computation.1 | async-start | bytes 32768 | tf_op jit(solution)/shard_map/all_to_all | solution.py:75
  23.8 7.0 %all-to-all-start = ((f32[32,32,256]{2,1,0:T(8,128)}), f32[32,32,256]{2,1,0:T(8,128)S(1)}, u32[]{:S(2)}, u32[]{:S(2)}) async-start(f32[32,32,256]{2,1,0:T(8,128)} %bitcast.7), calls=%async_computation | async-start | bytes 2097152 | tf_op jit(solution)/shard_map/all_to_all | solution.py:74
  30.9 5.6 %copy.19 = f32[1,1,256,4096]{2,3,1,0:T(8,128)} copy(f32[1,1,256,4096]{3,2,1,0:T(8,128)} %param.15) | data formatting | bytes 8388608 | tf_op args[2]
  36.6 4.4 %sort.35 = (s32[1024]{0:T(1024)}, s32[1024]{0:T(1024)S(1)}) sort(s32[1024]{0:T(1024)S(1)} %sub.21, s32[1024]{0:T(1024)S(1)} %iota.27), dimensions={0}, to_apply=%region_1.2 | sort | flops 10240 | bytes 16384 | tf_op jit(solution)/shard_map/jit(argsort)/sort | solution.py:78
  41.0 13.7 %all-to-all-done = f32[32,32,256]{2,1,0:T(8,128)S(1)} async-done(((f32[32,32,256]{2,1,0:T(8,128)}), f32[32,32,256]{2,1,0:T(8,128)S(1)}, u32[]{:S(2)}, u32[]{:S(2)}) %all-to-all-start) | async-done | bytes 1048608 | tf_op jit(solution)/shard_map/all_to_all | solution.py:74
  54.7 3.5 gather_fusion.4
  58.4 92.8 %while.26 = (s32[]{:T(128)}, f32[32,64,256]{2,1,0:T(8,128)S(1)}, s32[256]{0:T(256)S(1)}, s32[]{:T(128)}, f32[256,4096]{0,1:T(8,128)}, /*index=5*/s32[256]{0:T(25...) while((s32[]{:T(128)}, f32[32,64,256]{2,1,0:T(8,128)S(1)}, ...), condition=%wide.region_4.5_spmd, body=%wide.region_2.4_spmd.sunk | while | flops 1613236224 | bytes 69214120 | solution.py:35
  59.3 3.1 dynamic-slice_select_fusion.4
  62.4 5.6 %copy.22 = f32[128,64,64]{2,1,0:T(8,128)} copy(f32[128,64,64]{0,2,1:T(8,128)} %bitcast.40) | data formatting | bytes 4194304 | tf_op jit(solution)/shard_map/while/body/eval_jaxpr/reshape | solution.py:31
  68.0 4.3 %gather_fusion = f32[128,64,256]{2,1,0:T(8,128)} fusion(f32[16,64,256]{2,1,0:T(8,128)S(1)} %get-tuple-element.415, s32[1024]{0:T(1024)S(1)} %pad_clamp_fusion.5), kind=kCustom, calls=%fused_computation.clone.1 | custom fusion | bytes 16777728 | tf_op jit(solution)/shard_map/while/body/eval_jaxpr/gather | solution.py:32
  72.3 15.5 %fusion.25 = f32[128,64,256]{2,1,0:T(8,128)} fusion(f32[128,64,64]{2,1,0:T(8,128)} %copy.22, f32[128,64,256]{2,1,0:T(8,128)} %gather_fusion), kind=kOutput, calls=%fused_computation.33.clone.1 | convolution fusion | flops 1610612736 | bytes 18874368 | tf_op jit(solution)/shard_map/while/body/eval_jaxpr/kab,kbf->kaf/dot_general | solution.py:32
  87.8 17.1 %scatter_fusion = f32[32,64,256]{2,1,0:T(8,128)S(1)} fusion(f32[32,64,256]{2,1,0:T(8,128)S(1)} %get-tuple-element.399, s32[128]{0:T(128)S(1)} %get-tuple-element.376, f32[128,64,256]{2,1,0:T(8,128)} %fusion.25), kind=kCustom, calls=%fused_computation.5.clone.1 | custom fusion | flops 2097152 | bytes 25166336 | tf_op jit(solution)/shard_map/while/body/eval_jaxpr/scatter-add | solution.py:33
  105.6 3.1 dynamic-slice_select_fusion.4
  108.7 5.6 %copy.22 = f32[128,64,64]{2,1,0:T(8,128)} copy(f32[128,64,64]{0,2,1:T(8,128)} %bitcast.40) | data formatting | bytes 4194304 | tf_op jit(solution)/shard_map/while/body/eval_jaxpr/reshape | solution.py:31
  114.3 4.3 %gather_fusion = f32[128,64,256]{2,1,0:T(8,128)} fusion(f32[16,64,256]{2,1,0:T(8,128)S(1)} %get-tuple-element.415, s32[1024]{0:T(1024)S(1)} %pad_clamp_fusion.5), kind=kCustom, calls=%fused_computation.clone.1 | custom fusion | bytes 16777728 | tf_op jit(solution)/shard_map/while/body/eval_jaxpr/gather | solution.py:32
  118.6 15.5 %fusion.25 = f32[128,64,256]{2,1,0:T(8,128)} fusion(f32[128,64,64]{2,1,0:T(8,128)} %copy.22, f32[128,64,256]{2,1,0:T(8,128)} %gather_fusion), kind=kOutput, calls=%fused_computation.33.clone.1 | convolution fusion | flops 1610612736 | bytes 18874368 | tf_op jit(solution)/shard_map/while/body/eval_jaxpr/kab,kbf->kaf/dot_general | solution.py:32
  134.1 17.0 %scatter_fusion = f32[32,64,256]{2,1,0:T(8,128)S(1)} fusion(f32[32,64,256]{2,1,0:T(8,128)S(1)} %get-tuple-element.399, s32[128]{0:T(128)S(1)} %get-tuple-element.376, f32[128,64,256]{2,1,0:T(8,128)} %fusion.25), kind=kCustom, calls=%fused_computation.5.clone.1 | custom fusion | flops 2097152 | bytes 25166336 | tf_op jit(solution)/shard_map/while/body/eval_jaxpr/scatter-add | solution.py:33
  152.6 41.6 %reduce-scatter.3.cloned.1.call-done = f32[256,256]{1,0:T(8,128)} async-done(((f32[2048,256]{1,0:T(8,128)}), f32[256,256]{1,0:T(8,128)}) %reduce-scatter.3.cloned.1.call-update) | async-done | bytes 262160 | tf_op jit(solution)/shard_map/reduce_scatter | solution.py:94
  200.2 25.9 %all-gather.2.cloned.1.call-done = f32[2048,256]{1,0:T(8,128)} async-done(((f32[256,256]{1,0:T(8,128)}), f32[2048,256]{1,0:T(8,128)}) %all-gather.2.cloned.1.call-update) | async-done | bytes 2097168 | tf_op jit(solution)/shard_map/all_gather | solution.py:100
  226.2 93.1 %while.27 = (s32[]{:T(128)}, f32[16,64,256]{2,1,0:T(8,128)S(1)}, s32[256]{0:T(256)S(1)}, s32[]{:T(128)}, f32[256,4096]{0,1:T(8,128)}, /*index=5*/s32[256]{0:T(25...) while((s32[]{:T(128)}, f32[16,64,256]{2,1,0:T(8,128)S(1)}, ...), condition=%wide.region_8.9_spmd, body=%wide.region_6.8_spmd.sunk | while | flops 1613236224 | bytes 77602760 | solution.py:35
  230.0 5.8 %copy.23 = f32[128,64,64]{1,2,0:T(8,128)} copy(f32[128,64,64]{0,2,1:T(8,128)} %bitcast.41) | data formatting | bytes 4194304 | tf_op jit(solution)/shard_map/while/body/eval_jaxpr/reshape | solution.py:31
  235.8 4.3 %gather_fusion.1 = f32[128,64,256]{2,1,0:T(8,128)} fusion(f32[32,64,256]{2,1,0:T(8,128)S(1)} %copy-done.3, s32[1024]{0:T(1024)S(1)} %pad_clamp_fusion.6), kind=kCustom, calls=%fused_computation.1.clone.1 | custom fusion | bytes 16777728 | tf_op jit(solution)/shard_map/while/body/eval_jaxpr/gather | solution.py:32
  240.1 15.5 %fusion.28 = f32[128,64,256]{2,1,0:T(8,128)} fusion(f32[128,64,64]{1,2,0:T(8,128)} %copy.23, f32[128,64,256]{2,1,0:T(8,128)} %gather_fusion.1), kind=kOutput, calls=%fused_computation.34.clone.1 | convolution fusion | flops 1610612736 | bytes 18874368 | tf_op jit(solution)/shard_map/while/body/eval_jaxpr/kba,kbf->kaf/dot_general | solution.py:32
  255.7 17.1 %scatter_fusion.1 = f32[16,64,256]{2,1,0:T(8,128)S(1)} fusion(f32[16,64,256]{2,1,0:T(8,128)S(1)} %get-tuple-element.432, s32[128]{0:T(128)S(1)} %get-tuple-element.385, f32[128,64,256]{2,1,0:T(8,128)} %fusion.28), kind=kCustom, calls=%fused_computation.6.clone.1 | custom fusion | flops 2097152 | bytes 25166336 | tf_op jit(solution)/shard_map/while/body/eval_jaxpr/scatter-add | solution.py:33
  273.4 3.1 dynamic-slice_select_fusion.5
  276.5 5.8 %copy.23 = f32[128,64,64]{1,2,0:T(8,128)} copy(f32[128,64,64]{0,2,1:T(8,128)} %bitcast.41) | data formatting | bytes 4194304 | tf_op jit(solution)/shard_map/while/body/eval_jaxpr/reshape | solution.py:31
  282.4 4.3 %gather_fusion.1 = f32[128,64,256]{2,1,0:T(8,128)} fusion(f32[32,64,256]{2,1,0:T(8,128)S(1)} %copy-done.3, s32[1024]{0:T(1024)S(1)} %pad_clamp_fusion.6), kind=kCustom, calls=%fused_computation.1.clone.1 | custom fusion | bytes 16777728 | tf_op jit(solution)/shard_map/while/body/eval_jaxpr/gather | solution.py:32
  286.7 15.5 %fusion.28 = f32[128,64,256]{2,1,0:T(8,128)} fusion(f32[128,64,64]{1,2,0:T(8,128)} %copy.23, f32[128,64,256]{2,1,0:T(8,128)} %gather_fusion.1), kind=kOutput, calls=%fused_computation.34.clone.1 | convolution fusion | flops 1610612736 | bytes 18874368 | tf_op jit(solution)/shard_map/while/body/eval_jaxpr/kba,kbf->kaf/dot_general | solution.py:32
  302.2 17.1 %scatter_fusion.1 = f32[16,64,256]{2,1,0:T(8,128)S(1)} fusion(f32[16,64,256]{2,1,0:T(8,128)S(1)} %get-tuple-element.432, s32[128]{0:T(128)S(1)} %get-tuple-element.385, f32[128,64,256]{2,1,0:T(8,128)} %fusion.28), kind=kCustom, calls=%fused_computation.6.clone.1 | custom fusion | flops 2097152 | bytes 25166336 | tf_op jit(solution)/shard_map/while/body/eval_jaxpr/scatter-add | solution.py:33
  320.3 37.9 %psum.15 = f32[256]{0:T(256)S(1)} all-reduce(f32[256]{0:T(256)S(1)} %get-tuple-element.286), channel_id=1, replica_groups=mesh['row'=8,'col'=4] {'row','col'}, use_global_device_ids=true, to_apply=%region_12.13 | all-reduce | flops 256 | bytes 2048 | tf_op jit(solution)/shard_map/psum | solution.py:118
  360.4 23.6 %reduce-scatter.5.cloned.1.call-done = f32[256,256]{1,0:T(8,128)} async-done(((f32[1024,256]{1,0:T(8,128)}), f32[256,256]{1,0:T(8,128)}) %reduce-scatter.5.cloned.1.call-update) | async-done | bytes 262160 | tf_op jit(solution)/shard_map/reduce_scatter | solution.py:113
  (60 shorter events, 24.4 us)
Async XLA Ops:
  7.2 187.1 %copy-start = (f32[256,256]{1,0:T(8,128)S(1)}, f32[256,256]{1,0:T(8,128)}, u32[]{:S(2)}) copy-start(f32[256,256]{1,0:T(8,128)} %param.19) | copy-start | bytes 786436
  13.8 8.9 %all-to-all-start.1 = ((f32[32,1,32]{2,1,0:T(1,128)}), f32[32,1,32]{2,1,0:T(1,128)S(1)}, u32[]{:S(2)}, u32[]{:S(2)}) async-start(f32[32,1,32]{2,1,0:T(1,128)} %bitcast.9), calls=%async_computation.1 | async-start | bytes 32768 | tf_op jit(solution)/shard_map/all_to_all | solution.py:75
  23.8 30.9 %all-to-all-start = ((f32[32,32,256]{2,1,0:T(8,128)}), f32[32,32,256]{2,1,0:T(8,128)S(1)}, u32[]{:S(2)}, u32[]{:S(2)}) async-start(f32[32,32,256]{2,1,0:T(8,128)} %bitcast.7), calls=%async_computation | async-start | bytes 2097152 | tf_op jit(solution)/shard_map/all_to_all | solution.py:74
  30.8 163.4 %reduce-scatter.3.cloned.1.call-start = ((), (), s32[]{:S(2)}) async-start(), calls=%async_computation.4 | async-start | bytes 2359296 | tf_op jit(solution)/shard_map/reduce_scatter | solution.py:94
  54.7 3.7 copy-start.4
  54.7 3.7 copy-start.5
  58.4 135.9 %copy-start.6 = (f32[256]{0:T(256)S(1)}, f32[256]{0:T(256)}, u32[]{:S(2)}) copy-start(f32[256]{0:T(256)} %param.20) | copy-start | bytes 3076
  151.2 1.4 copy-start.2
  152.6 73.5 %all-gather.2.cloned.1.call-start = ((), (), s32[]{:S(2)}) async-start(), calls=%async_computation.5 | async-start | bytes 2359296 | tf_op jit(solution)/shard_map/all_gather | solution.py:100
  197.6 161.2 %all-reduce.2.cloned.1.call-start = ((), (), s32[]{:S(2)}) async-start(), calls=%async_computation.7 | async-start | bytes 524288 | tf_op jit(solution)/shard_map/psum | solution.py:118
  200.1 183.9 %reduce-scatter.5.cloned.1.call-start = ((), (), s32[]{:S(2)}) async-start(), calls=%async_computation.6 | async-start | bytes 1310720 | tf_op jit(solution)/shard_map/reduce_scatter | solution.py:113
  230.0 5.9 %copy-start.3 = (f32[32,64,256]{2,1,0:T(8,128)S(1)}, f32[32,64,256]{2,1,0:T(8,128)}, u32[]{:S(2)}) copy-start(f32[32,64,256]{2,1,0:T(8,128)} %get-tuple-element.448) | copy-start | bytes 6291460 | tf_op jit(solution)/shard_map/while
  276.5 5.9 %copy-start.3 = (f32[32,64,256]{2,1,0:T(8,128)S(1)}, f32[32,64,256]{2,1,0:T(8,128)}, u32[]{:S(2)}) copy-start(f32[32,64,256]{2,1,0:T(8,128)} %get-tuple-element.448) | copy-start | bytes 6291460 | tf_op jit(solution)/shard_map/while
  319.3 1.0 copy-start.1
Sparse Core Ops, SparseCore 0:
  152.7 41.5 reduce-scatter.2
  197.7 28.3 all-gather.1
  233.1 121.8 all-reduce.1
  357.9 26.1 reduce-scatter.4
where the time goes:
time: 397 us; the launch traced here: 391 us
  waiting for transfers between devices  106 us (27%)
  other arithmetic  94.1 us (24%)
  matrix products  67.6 us (17%)
  local copies, waits for them, and re-layouts  57.5 us (14%)
  blocking collectives  37.9 us (10%)
  between operations  13.9 us (4%)
  starting transfers between devices  13.6 us (3%)
    scatter-add x4, other arithmetic, one_group(): return partial_sum.at[into_at].add(terms)  68.2 us
    dot_general x4, matrix products, one_group(): jnp.einsum(pattern, group_vals, source_blocks[from_at], precision=precise)  62 us
    reduce_scatter x1, waiting for transfers between devices, on_device(): lax.psum_scatter(partial_value, 'row', scatter_dimension=0, tiled=True)  41.6 us
    psum x1, blocking collectives, on_device(): grad_w, grad_b = lax.psum((local_w, local_b), ('row', 'col'))  37.9 us
    all_gather x1, waiting for transfers between devices, on_device(): column = lax.all_gather(grad_hidden, 'row', axis=0, tiled=True)  25.9 us
    reduce_scatter x1, waiting for transfers between devices, on_device(): lax.psum_scatter(partial_x.reshape(group_rows, feat_width), 'col', scatte...  23.6 us
    reshape x4, local copies, waits for them, and re-layouts, one_group(): group_vals = group_vals.reshape(group_size, block_size, block_size)  22.7 us
    gather x4, local copies, waits for them, and re-layouts, one_group(): source_blocks[from_at]  17.2 us
  transfers between devices with their start and end apart: 6, of which 5 were waited for; matrix products, arithmetic and copies ran while one was open for 28% of the time, Pallas kernels for 0%

commit v1 on v0

v1 whole, which is shorter than its diff:
```python
import math

import jax
import jax.numpy as jnp
from jax import lax
from jax.sharding import PartitionSpec as P

precise = lax.Precision.HIGHEST
three = lax.Precision.HIGH


def general(
    features,
    loader_perm,
    block_values,
    block_row,
    block_column,
    tile_count,
    weight,
    bias_vector,
    cotangent,
):
    node_dev, feat_width = features.shape
    row_devices = lax.axis_size("row")
    col_devices = lax.axis_size("col")
    devices = row_devices * col_devices
    row_index = lax.axis_index("row")
    group_rows = col_devices * node_dev
    tile_vals = block_values[0, 0]
    slots, entries = tile_vals.shape
    side = math.isqrt(entries)
    out_blocks = row_devices * node_dev // side
    in_blocks = group_rows // side
    per_group = node_dev // row_devices
    ordering = jnp.argsort(loader_perm // group_rows, stable=True)
    sent_rows = jnp.broadcast_to(
        features[ordering].reshape(row_devices, 1, per_group, feat_width),
        (row_devices, col_devices, per_group, feat_width),
    ).reshape(devices, per_group, feat_width)
    sent_ids = jnp.broadcast_to(
        loader_perm[ordering].astype(jnp.float32).reshape(row_devices, 1, per_group),
        (row_devices, col_devices, per_group),
    ).reshape(devices, per_group)
    got_rows, got_ids = (
        lax.all_to_all(sent_rows, ("row", "col"), split_axis=0, concat_axis=0, tiled=True),
        lax.all_to_all(sent_ids, ("row", "col"), split_axis=0, concat_axis=0, tiled=True),
    )
    spot = block_row[0, 0] * in_blocks + block_column[0, 0]
    alive = jnp.arange(slots, dtype=jnp.int32) < tile_count[0, 0]
    places = jnp.arange(out_blocks * in_blocks, dtype=jnp.int32)
    chosen = ((places[:, None] == spot[None, :]) & alive[None, :]).astype(jnp.float32)
    dense = jnp.dot(chosen, tile_vals, precision=three)
    dense = dense.reshape(out_blocks, in_blocks, side, side).transpose(0, 2, 1, 3)
    dense = dense.reshape(out_blocks * side, in_blocks * side)

    local_pos = got_ids.reshape(group_rows).astype(jnp.int32) - row_index * group_rows
    at = jnp.arange(group_rows, dtype=jnp.int32)
    panel = jnp.dot(
        (at[:, None] == local_pos[None, :]).astype(jnp.float32),
        got_rows.reshape(group_rows, feat_width),
        precision=precise,
    )
    partial_value = jnp.dot(dense, panel, precision=three)
    hidden = lax.psum_scatter(partial_value, "row", scatter_dimension=0, tiled=True)
    preact = jnp.dot(hidden, weight, precision=precise) + bias_vector
    squashed = jax.nn.sigmoid(preact)
    output = preact * squashed
    grad_pre = cotangent * squashed * (1.0 + preact * (1.0 - squashed))
    grad_hidden = jnp.dot(grad_pre, weight.T, precision=precise)
    column = lax.all_gather(grad_hidden, "row", axis=0, tiled=True)
    local_w = jnp.einsum("nf,ng->fg", hidden, grad_pre, precision=precise)
    local_b = jnp.sum(grad_pre, axis=0)
    grad_w, grad_b = lax.psum((local_w, local_b), ("row", "col"))
    partial_x = jnp.einsum("nm,nf->mf", dense, column, precision=three)
    grad_x = lax.psum_scatter(partial_x, "col", scatter_dimension=0, tiled=True)
    norm_scale = 1.0 / math.sqrt(node_dev * devices)
    return (output, grad_x, grad_w * norm_scale, grad_b * norm_scale)


def solution(mesh):
    in_specs = (
        P(("row", "col"), None),
        P(("row", "col")),
        P("row", "col", None, None),
        P("row", "col", None),
        P("row", "col", None),
        P("row", "col"),
        P(),
        P(),
        P(("row", "col"), None),
    )
    out_specs = (P(("row", "col"), None), P(("row", "col"), None), P(), P())
    return jax.shard_map(
        general, mesh=mesh, in_specs=in_specs, out_specs=out_specs, check_vma=False
    )
```

time: 397 us -> 315 us (0.79)
  other arithmetic: 94.1 us -> 6.23 us
  waiting for transfers between devices: 106 us -> 175 us
  local copies, waits for them, and re-layouts: 57.5 us -> 26 us
  matrix products: 67.6 us -> 36.2 us
    psum x1, waiting for transfers between devices: 0.01 us -> 78.8 us  [general(): grad_w, grad_b = lax.psum((local_w, local_b), ('row', 'col'))]
    scatter-add x4 -> x0, other arithmetic: 68.2 us -> none  [one_group(): return partial_sum.at[into_at].add(terms)]
    dot_general x7, matrix products: 67.6 us -> 36.2 us  [the longest x1 11.7 us: general(): partial_x = jnp.einsum('nm,nf->mf', dense, column, precision=three)]
    gather x7 -> x2, local copies, waits for them, and re-layouts: 24.6 us -> 3.9 us  [the longest x1 1.98 us: general(): loader_perm[ordering].astype(jnp.float32).reshape(row_devices, 1, per_group)]
    all_to_all x2, waiting for transfers between devices: 14.5 us -> 0.82 us  [the longest x1 0.82 us: general(): lax.all_to_all(sent_ids, ('row', 'col'), split_axis=0, concat_axis=0, til...]
    select_n x10 -> x2, other arithmetic: 13.4 us -> 0.73 us  [the longest x1 0.73 us: general(): ordering = jnp.argsort(loader_perm // group_rows, stable=True)]
    reshape x4 -> x1, local copies, waits for them, and re-layouts: 22.7 us -> 14.5 us  [general(): dense = dense.reshape(out_blocks * side, in_blocks * side)]
    sort x2 -> x1, other arithmetic: 7.54 us -> 3.17 us  [general(): ordering = jnp.argsort(loader_perm // group_rows, stable=True)]
  transfers between devices with their start and end apart: 6 -> 6, of which waited for: 5 -> 5; matrix products, arithmetic and copies ran while one was open for 28% -> 16% of each run, Pallas kernels for 0% -> 0%
where the time goes in v1:
time: 315 us; the launch traced here: 309 us
  waiting for transfers between devices  175 us (56%)
  blocking collectives  37.9 us (12%)
  matrix products  36.2 us (11%)
  local copies, waits for them, and re-layouts  26 us (8%)
  between operations  14.5 us (5%)
  starting transfers between devices  13.5 us (4%)
  other arithmetic  6.23 us (2%)
    psum x1, waiting for transfers between devices, general(): grad_w, grad_b = lax.psum((local_w, local_b), ('row', 'col'))  78.8 us
    reduce_scatter x1, waiting for transfers between devices, general(): lax.psum_scatter(partial_value, 'row', scatter_dimension=0, tiled=True)  41.9 us
    psum x1, blocking collectives, general(): grad_w, grad_b = lax.psum((local_w, local_b), ('row', 'col'))  37.9 us
    reduce_scatter x1, waiting for transfers between devices, general(): grad_x = lax.psum_scatter(partial_x, 'col', scatter_dimension=0, tiled=True)  27.3 us
    all_gather x1, waiting for transfers between devices, general(): column = lax.all_gather(grad_hidden, 'row', axis=0, tiled=True)  26 us
    reshape x1, local copies, waits for them, and re-layouts, general(): dense = dense.reshape(out_blocks * side, in_blocks * side)  14.5 us
    dot_general x1, matrix products, general(): partial_x = jnp.einsum('nm,nf->mf', dense, column, precision=three)  11.7 us
    dot_general x1, matrix products, general(): dense = jnp.dot(chosen, tile_vals, precision=three)  9.72 us
  transfers between devices with their start and end apart: 6, of which 5 were waited for; matrix products, arithmetic and copies ran while one was open for 16% of the time, Pallas kernels for 0%

profile of v1, /device:TPU:27, one launch (start us, length us, event | category | flops | bytes accessed | tf_op | source)
XLA Modules:
  0.0 309.3 jit_solution(2826295909008541087)
XLA Ops:
  7.2 0.7 and_select_fusion
  7.9 3.2 %sort.17 = (s32[256]{0:T(256)}, s32[256]{0:T(256)S(1)}) sort(s32[256]{0:T(256)S(1)} %and_select_fusion, s32[256]{0:T(256)S(1)} %iota.27), dimensions={0}, to_apply=%region_0.1 | sort | flops 2048 | bytes 4096 | tf_op jit(solution)/shard_map/jit(argsort)/sort | solution.py:35
  11.1 2.0 gather_fusion
  13.1 0.1 convert_element_type.21
  13.2 0.6 broadcast_in_dim.9
  13.8 6.2 %all-to-all-start = ((f32[32,1,32]{2,1,0:T(1,128)}), f32[32,1,32]{2,1,0:T(1,128)S(1)}, u32[]{:S(2)}, u32[]{:S(2)}) async-start(f32[32,1,32]{2,1,0:T(1,128)} %bitcast.9), calls=%async_computation | async-start | bytes 32768 | tf_op jit(solution)/shard_map/all_to_all | solution.py:46
  20.0 1.9 gather_fusion.1
  21.9 0.8 all-to-all-done
  22.7 1.2 broadcast_in_dim.11
  23.9 7.0 %all-to-all-start.1 = ((f32[32,32,256]{2,1,0:T(8,128)}), f32[32,32,256]{2,1,0:T(8,128)S(1)}, u32[]{:S(2)}, u32[]{:S(2)}) async-start(f32[32,32,256]{2,1,0:T(8,128)} %bitcast.11), calls=%async_computation.1 | async-start | bytes 2097152 | tf_op jit(solution)/shard_map/all_to_all | solution.py:45
  30.9 0.0 reduce-scatter.3.cloned.1.call-start
  31.0 5.6 %copy.15 = f32[1,1,256,4096]{2,3,1,0:T(8,128)} copy(f32[1,1,256,4096]{3,2,1,0:T(8,128)} %param.11) | data formatting | bytes 8388608 | tf_op args[2]
  37.3 9.7 %convolution_bitcast_fusion = f32[32,64,16,64]{3,2,1,0:T(8,128)} fusion(f32[64,64,256,1]{2,1,0,3:T(8,128)} %bitcast.35, s32[256]{0:T(256)S(1)} %bitcast.38, s32[32,16]{1,0:T(8,128)S(1)} %multiply_add_fusion, pred[256]{0:T(512)(128)(4,1)S(1)} %iota_compare_fusion.2), kind=kOutput, calls=%fused_computation.2 | convolution fusion | flops 3221487616 | bytes 12586240 | tf_op jit(solution)/shard_map/dot_general | solution.py:52
  47.0 14.5 %reshape.85 = f32[2048,1024]{1,0:T(8,128)} reshape(f32[32,64,16,64]{3,2,1,0:T(8,128)} %convolution_bitcast_fusion) | data formatting | bytes 16777216 | tf_op jit(solution)/shard_map/reshape | solution.py:54
  61.5 0.1 subtract_reduce_fusion
  61.6 0.1 sub.25
  61.6 2.1 fusion
  63.8 7.2 %fusion.10 = f32[2048,256]{1,0:T(8,128)} fusion(f32[2048,1024]{1,0:T(8,128)} %reshape.85, f32[1024,256]{1,0:T(8,128)S(1)} %fusion), kind=kOutput, calls=%fused_computation.29 | convolution fusion | flops 3221225472 | bytes 11534336 | tf_op jit(solution)/shard_map/dot_general | solution.py:63
  71.1 0.0 all-gather.2.cloned.1.call-start
  71.1 41.9 %reduce-scatter.3.cloned.1.call-done = f32[256,256]{1,0:T(8,128)} async-done(((f32[2048,256]{1,0:T(8,128)}), f32[256,256]{1,0:T(8,128)}) %reduce-scatter.3.cloned.1.call-update) | async-done | bytes 262160 | tf_op jit(solution)/shard_map/reduce_scatter | solution.py:64
  113.0 2.1 fusion.9
  115.1 1.1 fusion.11
  116.3 0.0 all-reduce.2.cloned.1.call-start
  116.3 2.3 fusion.13
  118.6 0.2 reduce-scatter.5.cloned.1.call-start
  118.8 26.0 %all-gather.2.cloned.1.call-done = f32[2048,256]{1,0:T(8,128)} async-done(((f32[256,256]{1,0:T(8,128)}), f32[2048,256]{1,0:T(8,128)}) %all-gather.2.cloned.1.call-update) | async-done | bytes 2097168 | tf_op jit(solution)/shard_map/all_gather | solution.py:70
  144.8 11.7 %fusion.12 = f32[1024,256]{1,0:T(8,128)} fusion(f32[2048,1024]{1,0:T(8,128)} %reshape.85, f32[2048,256]{1,0:T(8,128)} %all-gather.2.cloned.1.call-done), kind=kOutput, calls=%fused_computation.31 | convolution fusion | flops 3221225472 | bytes 11534336 | tf_op jit(solution)/shard_map/nm,nf->mf/dot_general | solution.py:74
  156.5 37.9 %psum.15 = f32[256]{0:T(256)S(1)} all-reduce(f32[256]{0:T(256)S(1)} %get-tuple-element.6), channel_id=1, replica_groups=mesh['row'=8,'col'=4] {'row','col'}, use_global_device_ids=true, to_apply=%region_5.6 | all-reduce | flops 256 | bytes 2048 | tf_op jit(solution)/shard_map/psum | solution.py:73
  194.4 0.6 broadcast_multiply_fusion.1
  194.9 78.8 %all-reduce.2.cloned.1.call-done = f32[256,256]{1,0:T(8,128)} async-done(((f32[256,256]{1,0:T(8,128)}), f32[256,256]{1,0:T(8,128)}) %all-reduce.2.cloned.1.call-update) | async-done | bytes 262160 | tf_op jit(solution)/shard_map/psum | solution.py:73
  273.7 1.7 broadcast_multiply_fusion
  275.4 27.3 %reduce-scatter.5.cloned.1.call-done = f32[256,256]{1,0:T(8,128)} async-done(((f32[1024,256]{1,0:T(8,128)}), f32[256,256]{1,0:T(8,128)}) %reduce-scatter.5.cloned.1.call-update) | async-done | bytes 262160 | tf_op jit(solution)/shard_map/reduce_scatter | solution.py:75
  (22 shorter events, 0.1 us)
Async XLA Ops:
  7.2 105.8 %copy-start = (f32[256,256]{1,0:T(8,128)S(1)}, f32[256,256]{1,0:T(8,128)}, u32[]{:S(2)}) copy-start(f32[256,256]{1,0:T(8,128)} %param.15) | copy-start | bytes 786436
  13.8 8.9 %all-to-all-start = ((f32[32,1,32]{2,1,0:T(1,128)}), f32[32,1,32]{2,1,0:T(1,128)S(1)}, u32[]{:S(2)}, u32[]{:S(2)}) async-start(f32[32,1,32]{2,1,0:T(1,128)} %bitcast.9), calls=%async_computation | async-start | bytes 32768 | tf_op jit(solution)/shard_map/all_to_all | solution.py:46
  23.9 37.7 %all-to-all-start.1 = ((f32[32,32,256]{2,1,0:T(8,128)}), f32[32,32,256]{2,1,0:T(8,128)S(1)}, u32[]{:S(2)}, u32[]{:S(2)}) async-start(f32[32,32,256]{2,1,0:T(8,128)} %bitcast.11), calls=%async_computation.1 | async-start | bytes 2097152 | tf_op jit(solution)/shard_map/all_to_all | solution.py:45
  30.9 82.1 %reduce-scatter.3.cloned.1.call-start = ((), (), s32[]{:S(2)}) async-start(), calls=%async_computation.4 | async-start | bytes 2359296 | tf_op jit(solution)/shard_map/reduce_scatter | solution.py:64
  31.0 6.3 %copy-start.1 = (s32[1,1,256]{2,1,0:T(1,128)S(1)}, s32[1,1,256]{2,1,0:T(1,128)}, u32[]{:S(2)}) copy-start(s32[1,1,256]{2,1,0:T(1,128)} %param.13) | copy-start | bytes 3076
  31.0 6.3 %copy-start.2 = (s32[1,1,256]{2,1,0:T(1,128)S(1)}, s32[1,1,256]{2,1,0:T(1,128)}, u32[]{:S(2)}) copy-start(s32[1,1,256]{2,1,0:T(1,128)} %param.12) | copy-start | bytes 3076
  63.8 49.2 %copy-start.3 = (f32[256,256]{1,0:T(8,128)S(1)}, f32[256,256]{1,0:T(8,128)}, u32[]{:S(2)}) copy-start(f32[256,256]{1,0:T(8,128)} %param.17) | copy-start | bytes 786436
  63.8 49.2 %copy-start.4 = (f32[256]{0:T(256)S(1)}, f32[256]{0:T(256)}, u32[]{:S(2)}) copy-start(f32[256]{0:T(256)} %param.16) | copy-start | bytes 3076
  71.1 73.7 %all-gather.2.cloned.1.call-start = ((), (), s32[]{:S(2)}) async-start(), calls=%async_computation.5 | async-start | bytes 2359296 | tf_op jit(solution)/shard_map/all_gather | solution.py:70
  116.3 157.5 %all-reduce.2.cloned.1.call-start = ((), (), s32[]{:S(2)}) async-start(), calls=%async_computation.7 | async-start | bytes 524288 | tf_op jit(solution)/shard_map/psum | solution.py:73
  118.6 184.1 %reduce-scatter.5.cloned.1.call-start = ((), (), s32[]{:S(2)}) async-start(), calls=%async_computation.6 | async-start | bytes 1310720 | tf_op jit(solution)/shard_map/reduce_scatter | solution.py:75
Sparse Core Ops, SparseCore 0:
  71.2 41.7 reduce-scatter.2
  116.4 28.3 all-gather.1
  151.8 121.8 all-reduce.1
  276.6 26.1 reduce-scatter.4

commit v2 on v1

--- a/solution.py
+++ b/solution.py
@@ -1,8 +1,11 @@
+import functools
 import math
 
 import jax
 import jax.numpy as jnp
 from jax import lax
+from jax.experimental import pallas as pl
+from jax.experimental.pallas import tpu as pltpu
 from jax.sharding import PartitionSpec as P
 
 precise = lax.Precision.HIGHEST
@@ -77,6 +80,433 @@
     return (output, grad_x, grad_w * norm_scale, grad_b * norm_scale)
 
 
+def fused(
+    node_dev, row_devices, col_devices, side,
+    ids_row, ids_col, blk_row, blk_col, live, feats, vals_hbm, weight, bias, cotan,
+    out, grad_x, grad_w, grad_b,
+    sorted_rows, sorted_ids, got, got_ids, vals, tall, tile_hi, tile_lo, panel_hi, panel_lo,
+    sent_part, core_part, summed, from_x, from_y, turned, late,
+    column, column_hi, column_lo, sent_x, came_x, w_sent, w_came, w_line, w_full,
+    vals_sem, fs, fr, fis, fir, zs, zr, zis, zir, cs, cr, xs, xr, ys, yr, ls, lr,
+    ags, agr, ds, dr, ks, kr, gs, gr, ws, wr, wls, wlr, wfs, wfr,
+):
+    width = weight.shape[0]
+    row, col = lax.axis_index("row"), lax.axis_index("col")
+    core, chip = row % 2, row // 2
+    x, y = chip % 2, chip // 2
+    at_core = row + 1 - 2 * core
+    at_x = row + 2 - 4 * x
+    at_y = row + 4 - 8 * y
+    at_diag = at_x + 4 - 8 * y
+    half = node_dev // 2
+    group_rows = col_devices * node_dev
+    per = node_dev // row_devices
+    slots = vals.shape[0]
+    f32, bf16 = jnp.float32, jnp.bfloat16
+
+    def remote(src, dst, ssem, rsem, **where):
+        return pltpu.make_async_remote_copy(
+            src_ref=src, dst_ref=dst, send_sem=ssem, recv_sem=rsem,
+            device_id=where, device_id_type=pl.DeviceIdType.MESH,
+        )
+
+    def dot(a, b):
+        return jnp.dot(a, b, preferred_element_type=f32)
+
+    def exact(a, b):
+        return jnp.dot(a, b, precision=precise, preferred_element_type=f32)
+
+    def split(a):
+        hi = a.astype(bf16)
+        return hi, (a - hi.astype(f32)).astype(bf16)
+
+    fetch = pltpu.make_async_copy(vals_hbm, vals, vals_sem)
+    fetch.start()
+
+    barrier = pltpu.get_barrier_semaphore()
+    for t in range(1, row_devices):
+        pl.semaphore_signal(
+            barrier, inc=1, device_id={"row": (row + t) % row_devices},
+            device_id_type=pl.DeviceIdType.MESH,
+        )
+    for t in range(1, col_devices):
+        pl.semaphore_signal(
+            barrier, inc=1, device_id={"col": (col + t) % col_devices},
+            device_id_type=pl.DeviceIdType.MESH,
+        )
+
+    idr, idc = ids_row[...], ids_col[...]
+    scale = 1.0 / group_rows
+    grp_r, grp_c = jnp.floor(idr * scale), jnp.floor(idc * scale)
+    sub = lax.broadcasted_iota(jnp.int32, (node_dev, node_dev), 0)
+    lane = lax.broadcasted_iota(jnp.int32, (node_dev, node_dev), 1)
+    same = grp_c == grp_r
+    rank_r = jnp.sum(jnp.where(same & (sub < lane), 1.0, 0.0), axis=0, keepdims=True)
+    rank_c = jnp.sum(jnp.where(same & (lane < sub), 1.0, 0.0), axis=1, keepdims=True)
+    slot_r = grp_r * per + rank_r
+    order = jnp.where(sub.astype(f32) == slot_r, 1.0, 0.0)
+    moved = exact(order, feats[...])
+    packed = 128 // per
+    lane128 = lax.broadcasted_iota(jnp.int32, (node_dev, 128), 1)
+    shift = ((row % packed) * per).astype(f32)
+    placed = jnp.where(lane128.astype(f32) == rank_c + shift, 1.0, 0.0)
+    dest = lax.broadcasted_iota(jnp.int32, (row_devices, node_dev), 0).astype(f32)
+    id_rows = exact(jnp.where(dest == grp_r, idr, 0.0), placed)
+    for d in range(row_devices):
+        sorted_rows[d] = moved[d * per:(d + 1) * per]
+        sorted_ids[d] = id_rows[d:d + 1]
+    got[col, row] = sorted_rows[row]
+    got_ids[col, row] = sorted_ids[row]
+
+    pl.semaphore_wait(barrier, row_devices - 1 + col_devices - 1)
+    first = []
+    for t in range(1, row_devices):
+        to = (row + t) % row_devices
+        a = remote(sorted_rows.at[to], got.at[col, row], fs.at[t], fr.at[t], row=to)
+        b = remote(sorted_ids.at[to], got_ids.at[col, row], fis.at[t], fir.at[t], row=to)
+        a.start()
+        b.start()
+        first += [a, b]
+
+    fetch.wait()
+
+    count = live[...]
+    slot_at = lax.broadcasted_iota(jnp.int32, (1, slots), 1)
+    out_blocks = row_devices * node_dev // side
+    in_blocks = group_rows // side
+    key = jnp.where(slot_at < count, blk_col[...] * out_blocks + blk_row[...], -1)
+    spot = lax.broadcasted_iota(jnp.int32, (out_blocks * in_blocks, slots), 0)
+    chosen = jnp.where(spot == key, 1.0, 0.0).astype(bf16)
+    left = lax.broadcasted_iota(jnp.int32, (out_blocks, 128), 1) < side
+
+    def densify(step, carry):
+        part = vals[:, pl.ds(pl.multiple_of(step * 256, 256), 256)]
+        hi, lo = split(part)
+        dense = dot(chosen, hi) + dot(chosen, lo)
+        for pair in range(in_blocks // 2):
+            top = dense[(2 * pair) * out_blocks:(2 * pair + 1) * out_blocks]
+            low = dense[(2 * pair + 1) * out_blocks:(2 * pair + 2) * out_blocks]
+            for h in range(2):
+                p0, p1 = top[:, h * 128:(h + 1) * 128], low[:, h * 128:(h + 1) * 128]
+                even = jnp.where(left, p0, pltpu.roll(p1, side, 1))
+                odd = jnp.where(left, pltpu.roll(p0, side, 1), p1)
+                at = step * 4 + h * 2
+                tall[pair, pl.ds(at, out_blocks, stride=side), :] = even
+                tall[pair, pl.ds(at + 1, out_blocks, stride=side), :] = odd
+        return carry
+
+    steps = vals.shape[1] // 256
+    lax.fori_loop(0, steps // 2, densify, 0)
+
+    for t in range(1, row_devices):
+        frm = (row + row_devices - t) % row_devices
+        remote(sorted_rows.at[frm], got.at[col, frm], fs.at[t], fr.at[t], row=frm).wait_recv()
+        remote(sorted_ids.at[frm], got_ids.at[col, frm], fis.at[t], fir.at[t], row=frm).wait_recv()
+    second = []
+    for t in range(1, col_devices):
+        to = (col + t) % col_devices
+        a = remote(got.at[col], got.at[col], zs.at[t], zr.at[t], col=to)
+        b = remote(got_ids.at[col], got_ids.at[col], zis.at[t], zir.at[t], col=to)
+        a.start()
+        b.start()
+        second += [a, b]
+
+    lax.fori_loop(steps // 2, steps, densify, 0)
+
+    def narrow(i, carry):
+        at = pl.multiple_of(i * node_dev, node_dev)
+        for pair in range(in_blocks // 2):
+            hi, lo = split(tall[pair, pl.ds(at, node_dev), :])
+            tile_hi[pl.ds(at, node_dev), pair * 128:(pair + 1) * 128] = hi
+            tile_lo[pl.ds(at, node_dev), pair * 128:(pair + 1) * 128] = lo
+        return carry
+
+    lax.fori_loop(0, row_devices, narrow, 0)
+
+    for t in range(1, col_devices):
+        frm = (col + col_devices - t) % col_devices
+        remote(got.at[col], got.at[frm], zs.at[t], zr.at[t], col=frm).wait_recv()
+        remote(got_ids.at[col], got_ids.at[frm], zis.at[t], zir.at[t], col=frm).wait_recv()
+
+    pieces = []
+    for j in range(col_devices):
+        for s in range(0, row_devices, packed):
+            pieces.append(sum(got_ids[j, s + k] for k in range(packed)))
+    where = jnp.concatenate(pieces, axis=1) - (row * group_rows).astype(f32)
+    got_hi, got_lo = split(got[...].reshape(group_rows, width))
+
+    def place(i, carry):
+        at = pl.multiple_of(i * node_dev, node_dev)
+        here = lax.broadcasted_iota(jnp.int32, (node_dev, group_rows), 0) + at
+        pick = jnp.where(here.astype(f32) == where, 1.0, 0.0).astype(bf16)
+        panel_hi[pl.ds(at, node_dev), :] = dot(pick, got_hi).astype(bf16)
+        panel_lo[pl.ds(at, node_dev), :] = dot(pick, got_lo).astype(bf16)
+        return carry
+
+    lax.fori_loop(0, col_devices, place, 0)
+
+    def chunk(i):
+        at = pl.multiple_of(i * node_dev, node_dev)
+        a, b = tile_hi[pl.ds(at, node_dev), :], tile_lo[pl.ds(at, node_dev), :]
+        return dot(a, panel_hi[...]) + dot(a, panel_lo[...]) + dot(b, panel_hi[...])
+
+    def flipped(t):
+        fx, fy = 1 - t // 2, 1 - t % 2
+        return (y + fy - 2 * y * fy) * 2 + (x + fx - 2 * x * fx)
+
+    def core_copy(t):
+        return remote(sent_part.at[t], core_part.at[t], cs.at[t], cr.at[t], row=at_core)
+
+    def to_pair(t, carry):
+        sent_part[t] = chunk(flipped(t) * 2 + 1 - core)
+        core_copy(t).start()
+        return carry
+
+    lax.fori_loop(0, 4, to_pair, 0)
+
+    def x_copy(t):
+        f = 1 - t % 2
+        return remote(summed.at[t, pl.ds(0, half)], from_x.at[f], xs.at[f], xr.at[f], row=at_x)
+
+    def y_copy(t):
+        f = 1 - t // 2
+        return remote(summed.at[t, pl.ds(half, half)], from_y.at[f], ys.at[f], yr.at[f], row=at_y)
+
+    for t in range(4):
+        own = chunk(flipped(t) * 2 + core)
+        core_copy(t).wait_recv()
+        summed[t] = own + core_part[t]
+        if t < 2:
+            x_copy(t).start()
+        if t % 2 == 0:
+            y_copy(t).start()
+    x_copy(0).wait_recv()
+    turned[0] = summed[2, 0:half] + from_x[1]
+    late_y = remote(turned.at[0], late.at[0], ls.at[0], lr.at[0], row=at_y)
+    late_y.start()
+    y_copy(0).wait_recv()
+    turned[1] = summed[1, half:] + from_y[1]
+    late_x = remote(turned.at[1], late.at[1], ls.at[1], lr.at[1], row=at_x)
+    late_x.start()
+    x_copy(1).wait_recv()
+    y_copy(2).wait_recv()
+    late_y.wait_recv()
+    late_x.wait_recv()
+    hidden = jnp.concatenate(
+        [summed[3, 0:half] + from_x[0] + late[0], summed[3, half:] + from_y[0] + late[1]], axis=0
+    )
+
+    w = weight[...]
+    preact = exact(hidden, w) + bias[...]
+    squashed = jax.nn.sigmoid(preact)
+    out[...] = preact * squashed
+    grad_pre = cotan[...] * squashed * (1.0 + preact * (1.0 - squashed))
+    column[row] = lax.dot_general(
+        w, grad_pre, (((1,), (1,)), ((), ())), precision=precise, preferred_element_type=f32
+    )
+
+    def gather(k, frm, to):
+        return remote(column.at[frm], column.at[frm], ags.at[k], agr.at[k], row=to)
+
+    def diag(k, frm, to):
+        part = pl.ds(k * half, half)
+        return remote(column.at[frm, part], column.at[frm, part], ds.at[k], dr.at[k], row=to)
+
+    def pair(k, frm):
+        return remote(column.at[frm], column.at[frm], ks.at[k], kr.at[k], row=at_core)
+
+    other = 1 - 2 * core
+    sends = [gather(0, row, at_x), gather(1, row, at_y), pair(0, row)]
+    for c in sends:
+        c.start()
+
+    local_w = exact(hidden.T, grad_pre)
+    local_b = jnp.broadcast_to(jnp.sum(grad_pre, axis=0, keepdims=True), (8, width))
+    wper = width // row_devices
+    for d in range(row_devices):
+        w_sent[d, 0:wper] = local_w[d * wper:(d + 1) * wper]
+        w_sent[d, wper:] = local_b
+    w_came[row] = w_sent[row]
+
+    def narrowed(i):
+        hi, lo = split(column[i])
+        at = pl.multiple_of(i * node_dev, node_dev)
+        column_hi[:, pl.ds(at, node_dev)] = hi
+        column_lo[:, pl.ds(at, node_dev)] = lo
+
+    gather(1, at_y, at_y).wait_recv()
+    more = [diag(0, at_y, at_x), pair(1, at_y)]
+    for c in more:
+        c.start()
+    sends += more
+    gather(0, at_x, at_x).wait_recv()
+    more = [diag(1, at_x, at_y), pair(2, at_x)]
+    for c in more:
+        c.start()
+    sends += more
+    for t in range(1, row_devices):
+        to = (row + t) % row_devices
+        c = remote(w_sent.at[to], w_came.at[row], ws.at[t], wr.at[t], row=to)
+        c.start()
+        sends.append(c)
+    narrowed(row)
+    narrowed(at_y)
+    narrowed(at_x)
+    diag(0, at_diag, at_x).wait_recv()
+    diag(1, at_diag, at_y).wait_recv()
+    c = pair(3, at_diag)
+    c.start()
+    sends.append(c)
+    narrowed(at_diag)
+    for k, frm in enumerate((row, at_y, at_x, at_diag)):
+        pair(k, frm + other).wait_recv()
+        narrowed(frm + other)
+
+    def back(j):
+        at = pl.multiple_of(j * node_dev, node_dev)
+        a, b = tile_hi[:, pl.ds(at, node_dev)], tile_lo[:, pl.ds(at, node_dev)]
+        return dot(column_hi[...], a) + dot(column_lo[...], a) + dot(column_hi[...], b)
+
+    def x_line(t):
+        return remote(sent_x.at[t], came_x.at[t], gs.at[t], gr.at[t], col=(col + t + 1) % col_devices)
+
+    def to_line(t, carry):
+        sent_x[t] = back((col + t + 1) % col_devices)
+
+        @pl.when(t < col_devices - 1)
+        def _():
+            x_line(t).start()
+
+        return carry
+
+    lax.fori_loop(0, col_devices, to_line, 0)
+
+    for t in range(1, row_devices):
+        frm = (row + row_devices - t) % row_devices
+        remote(w_sent.at[frm], w_came.at[frm], ws.at[t], wr.at[t], row=frm).wait_recv()
+    total = w_came[0]
+    for s in range(1, row_devices):
+        total = total + w_came[s]
+    w_line[col] = total
+    for t in range(1, col_devices):
+        c = remote(w_line.at[col], w_line.at[col], wls.at[t], wlr.at[t], col=(col + t) % col_devices)
+        c.start()
+        sends.append(c)
+    for t in range(1, col_devices):
+        frm = (col + col_devices - t) % col_devices
+        remote(w_line.at[col], w_line.at[frm], wls.at[t], wlr.at[t], col=frm).wait_recv()
+    total = w_line[0]
+    for s in range(1, col_devices):
+        total = total + w_line[s]
+    norm_scale = 1.0 / math.sqrt(node_dev * row_devices * col_devices)
+    w_full[row] = total * norm_scale
+    for t in range(1, row_devices):
+        to = (row + t) % row_devices
+        c = remote(w_full.at[row], w_full.at[row], wfs.at[t], wfr.at[t], row=to)
+        c.start()
+        sends.append(c)
+    for t in range(1, row_devices):
+        frm = (row + row_devices - t) % row_devices
+        remote(w_full.at[row], w_full.at[frm], wfs.at[t], wfr.at[t], row=frm).wait_recv()
+    for d in range(row_devices):
+        grad_w[d * wper:(d + 1) * wper, :] = w_full[d, 0:wper]
+    grad_b[...] = w_full[0, wper:]
+
+    for t in range(col_devices - 1):
+        x_line(t).wait_recv()
+    total = sent_x[col_devices - 1]
+    for t in range(col_devices - 1):
+        total = total + came_x[t]
+    grad_x[...] = total.T
+
+    for c in first + second + sends:
+        c.wait_send()
+    for t in range(4):
+        core_copy(t).wait_send()
+    for t in (0, 1):
+        x_copy(t).wait_send()
+    for t in (0, 2):
+        y_copy(t).wait_send()
+    late_y.wait_send()
+    late_x.wait_send()
+    for t in range(col_devices - 1):
+        x_line(t).wait_send()
+
+
+def in_one_kernel(
+    features,
+    loader_perm,
+    block_values,
+    block_row,
+    block_column,
+    tile_count,
+    weight,
+    bias_vector,
+    cotangent,
+):
+    node_dev, width = features.shape
+    rows, cols = lax.axis_size("row"), lax.axis_size("col")
+    _, _, slots, entries = block_values.shape
+    side = math.isqrt(entries)
+    half, per = node_dev // 2, node_dev // rows
+    high, wide = rows * node_dev, cols * node_dev
+    wper = width // rows + 8
+    f32, bf16 = jnp.float32, jnp.bfloat16
+    ids = loader_perm.astype(f32)
+    vmem = pl.BlockSpec(memory_space=pltpu.VMEM)
+    dma = pltpu.SemaphoreType.DMA
+    V = pltpu.VMEM
+    square = (node_dev, width)
+    out, grad_x, grad_w, grad_b = pl.pallas_call(
+        functools.partial(fused, node_dev, rows, cols, side),
+        out_shape=(
+            jax.ShapeDtypeStruct(square, f32),
+            jax.ShapeDtypeStruct(square, f32),
+            jax.ShapeDtypeStruct((width, width), f32),
+            jax.ShapeDtypeStruct((8, width), f32),
+        ),
+        in_specs=[vmem] * 6 + [pl.BlockSpec(memory_space=pl.ANY)] + [vmem] * 3,
+        out_specs=(vmem,) * 4,
+        scratch_shapes=[
+            V((rows, per, width), f32), V((rows, 1, 128), f32),
+            V((cols, rows, per, width), f32), V((cols, rows, 1, 128), f32),
+            V((slots, entries), f32), V((wide // 128, high, 128), f32),
+            V((high, wide), bf16), V((high, wide), bf16),
+            V((wide, width), bf16), V((wide, width), bf16),
+            V((4,) + square, f32), V((4,) + square, f32), V((4,) + square, f32),
+            V((2, half, width), f32), V((2, half, width), f32),
+            V((2, half, width), f32), V((2, half, width), f32),
+            V((rows, width, node_dev), f32),
+            V((width, high), bf16), V((width, high), bf16),
+            V((cols, width, node_dev), f32), V((cols - 1, width, node_dev), f32),
+            V((rows, wper, width), f32), V((rows, wper, width), f32),
+            V((cols, wper, width), f32), V((rows, wper, width), f32),
+            dma,
+            dma((rows,)), dma((rows,)), dma((rows,)), dma((rows,)),
+            dma((cols,)), dma((cols,)), dma((cols,)), dma((cols,)),
+            dma((4,)), dma((4,)), dma((2,)), dma((2,)), dma((2,)), dma((2,)), dma((2,)), dma((2,)),
+            dma((2,)), dma((2,)), dma((2,)), dma((2,)), dma((4,)), dma((4,)),
+            dma((cols,)), dma((cols,)), dma((rows,)), dma((rows,)),
+            dma((cols,)), dma((cols,)), dma((rows,)), dma((rows,)),
+        ],
+        compiler_params=pltpu.CompilerParams(
+            collective_id=0, has_side_effects=True, vmem_limit_bytes=58 * 2**20
+        ),
+    )(
+        ids.reshape(1, node_dev),
+        ids.reshape(node_dev, 1),
+        block_row.reshape(1, slots),
+        block_column.reshape(1, slots),
+        tile_count,
+        features,
+        block_values.reshape(slots, entries),
+        weight,
+        bias_vector.reshape(1, width),
+        cotangent,
+    )
+    return (out, grad_x, grad_w, grad_b[0])
+
+
 def solution(mesh):
     in_specs = (
         P(("row", "col"), None),
@@ -90,6 +520,8 @@
         P(("row", "col"), None),
     )
     out_specs = (P(("row", "col"), None), P(("row", "col"), None), P(), P())
+    small = mesh.shape["row"] == 8 and mesh.shape["col"] == 4
     return jax.shard_map(
-        general, mesh=mesh, in_specs=in_specs, out_specs=out_specs, check_vma=False
-    )
+        in_one_kernel if small else general,
+        mesh=mesh, in_specs=in_specs, out_specs=out_specs, check_vma=False,
+    )

time: 315 us -> 109 us (0.35); the launches traced: 309 us -> 109 us
  waiting for transfers between devices: 175 us -> 0 us
  Pallas kernels: 0 us -> 99.6 us
  blocking collectives: 37.9 us -> 0 us
  matrix products: 36.2 us -> 0 us
  local copies, waits for them, and re-layouts: 26 us -> 7.07 us
  starting transfers between devices: 13.5 us -> 0 us
  between operations: 14.5 us -> 1.29 us
  other arithmetic: 6.23 us -> 0.68 us
    pallas_call x0 -> x1, Pallas kernels: none -> 99.6 us  [in_one_kernel(): pl.pallas_call(functools.partial(fused, node_dev, rows, cols, side), out_...]
    psum x1 -> x0, waiting for transfers between devices: 78.8 us -> none  [general(): grad_w, grad_b = lax.psum((local_w, local_b), ('row', 'col'))]
    reduce_scatter x2 -> x0, waiting for transfers between devices: 69.2 us -> none  [the longest x1 41.9 us: general(): lax.psum_scatter(partial_value, 'row', scatter_dimension=0, tiled=True)]
    psum x1 -> x0, blocking collectives: 37.9 us -> none  [general(): grad_w, grad_b = lax.psum((local_w, local_b), ('row', 'col'))]
    dot_general x7 -> x0, matrix products: 36.2 us -> none  [the longest x1 11.7 us: general(): partial_x = jnp.einsum('nm,nf->mf', dense, column, precision=three)]
    all_gather x1 -> x0, waiting for transfers between devices: 26 us -> none  [general(): column = lax.all_gather(grad_hidden, 'row', axis=0, tiled=True)]
    reshape x1, local copies, waits for them, and re-layouts: 14.5 us -> 0.8 us  [in_one_kernel(): ids.reshape(node_dev, 1)]
    all_to_all x2 -> x0, starting transfers between devices: 13.2 us -> none  [the longest x1 7 us: general(): lax.all_to_all(sent_rows, ('row', 'col'), split_axis=0, concat_axis=0, ti...]
  transfers between devices with their start and end apart: 6 -> 0, of which waited for: 5 -> 0; matrix products, arithmetic and copies ran while one was open for 16% -> 0% of each run, Pallas kernels for 0% -> 0%
where the time goes in v2:
time: 109 us
  Pallas kernels  99.6 us (91%)
  local copies, waits for them, and re-layouts  7.07 us (6%)
  between operations  1.29 us (1%)
    pallas_call x1, Pallas kernels, in_one_kernel(): pl.pallas_call(functools.partial(fused, node_dev, rows, cols, side), out_...  99.6 us
    unnamed x5, local copies, waits for them, and re-layouts  5.01 us

profile of v2, /device:TPU:27, one launch (start us, length us, event | category | flops | bytes accessed | tf_op | source)
XLA Modules:
  0.0 108.7 jit_solution(12420126389314623284)
XLA Ops:
  1.3 0.7 convert_element_type.3
  2.0 0.0 copy-start
  2.0 0.8 copy.13.ids_col
  2.8 0.0 copy-done
  2.8 99.6 %shard_map.120 = (f32[256,256]{1,0:T(8,128)}, f32[256,256]{1,0:T(8,128)}, f32[256,256]{1,0:T(8,128)}, f32[8,256]{1,0:T(8,128)}) custom-call(f32[1,256]{1,0:T(1,128)} %bitcast.9, f32[256,1]{1,0:T(8,128)} %copy.13.ids_col, s32[1,256]{1,0:T(1,128)} %bitcast.10, s32[1,256]{1,0:T(1,128)} %bitcast.11, s32[1,1]{1,0:T(1,128)S(6)} %copy.17.live, f32[256,256]{1,0:T(8,128)} %feats.1, ...), custom_call_target="tpu_custom_call" | custom-call | tf_op jit(solution)/shard_map/pallas_call | solution.py:460
  102.4 1.3 %slice.3 = f32[1,256]{1,0:T(1,128)} slice(f32[8,256]{1,0:T(8,128)} %get-tuple-element.11), slice={[0:1], [0:256]} | slice | bytes 2048 | tf_op jit(solution)/shard_map/slice | solution.py:507
  103.7 1.7 %copy.18 = f32[256,256]{1,0:T(8,128)} copy(f32[256,256]{1,0:T(8,128)} %get-tuple-element.16) | data formatting | bytes 524288
  105.4 1.7 %copy.19 = f32[256,256]{1,0:T(8,128)} copy(f32[256,256]{1,0:T(8,128)} %get-tuple-element.17) | data formatting | bytes 524288
  107.0 1.7 %copy.20 = f32[256,256]{1,0:T(8,128)} copy(f32[256,256]{1,0:T(8,128)} %get-tuple-element.18) | data formatting | bytes 524288
Async XLA Ops:
  2.0 0.8 copy-start

commit v3 on v2

--- a/solution.py
+++ b/solution.py
@@ -196,7 +196,7 @@
         return carry
 
     steps = vals.shape[1] // 256
-    lax.fori_loop(0, steps // 2, densify, 0)
+    lax.fori_loop(0, steps // 8, densify, 0)
 
     for t in range(1, row_devices):
         frm = (row + row_devices - t) % row_devices
@@ -211,7 +211,7 @@
         b.start()
         second += [a, b]
 
-    lax.fori_loop(steps // 2, steps, densify, 0)
+    lax.fori_loop(steps // 8, steps, densify, 0)
 
     def narrow(i, carry):
         at = pl.multiple_of(i * node_dev, node_dev)
@@ -379,8 +379,6 @@
 
         return carry
 
-    lax.fori_loop(0, col_devices, to_line, 0)
-
     for t in range(1, row_devices):
         frm = (row + row_devices - t) % row_devices
         remote(w_sent.at[frm], w_came.at[frm], ws.at[t], wr.at[t], row=frm).wait_recv()
@@ -392,6 +390,8 @@
         c = remote(w_line.at[col], w_line.at[col], wls.at[t], wlr.at[t], col=(col + t) % col_devices)
         c.start()
         sends.append(c)
+    lax.fori_loop(0, col_devices, to_line, 0)
+
     for t in range(1, col_devices):
         frm = (col + col_devices - t) % col_devices
         remote(w_line.at[col], w_line.at[frm], wls.at[t], wlr.at[t], col=frm).wait_recv()
@@ -410,7 +410,7 @@
         remote(w_full.at[row], w_full.at[frm], wfs.at[t], wfr.at[t], row=frm).wait_recv()
     for d in range(row_devices):
         grad_w[d * wper:(d + 1) * wper, :] = w_full[d, 0:wper]
-    grad_b[...] = w_full[0, wper:]
+    grad_b[...] = w_full[0, wper:wper + 1]
 
     for t in range(col_devices - 1):
         x_line(t).wait_recv()
@@ -463,7 +463,7 @@
             jax.ShapeDtypeStruct(square, f32),
             jax.ShapeDtypeStruct(square, f32),
             jax.ShapeDtypeStruct((width, width), f32),
-            jax.ShapeDtypeStruct((8, width), f32),
+            jax.ShapeDtypeStruct((1, width), f32),
         ),
         in_specs=[vmem] * 6 + [pl.BlockSpec(memory_space=pl.ANY)] + [vmem] * 3,
         out_specs=(vmem,) * 4,
@@ -504,7 +504,7 @@
         bias_vector.reshape(1, width),
         cotangent,
     )
-    return (out, grad_x, grad_w, grad_b[0])
+    return (out, grad_x, grad_w, grad_b.reshape(width))
 
 
 def solution(mesh):

time: 109 us -> 101 us (0.927)
  Pallas kernels: 99.6 us -> 91.5 us
    pallas_call x1, Pallas kernels: 99.6 us -> 91.5 us  [in_one_kernel(): pl.pallas_call(functools.partial(fused, node_dev, rows, cols, side), out_...]
    slice x1 -> x0, local copies, waits for them, and re-layouts: 1.26 us -> none  [in_one_kernel(): return (out, grad_x, grad_w, grad_b[0])]
    unnamed x5 -> x6, local copies, waits for them, and re-layouts: 5.01 us -> 6.23 us
where the time goes in v3:
time: 101 us
  Pallas kernels  91.5 us (91%)
  local copies, waits for them, and re-layouts  7.03 us (7%)
  between operations  1.29 us (1%)
    pallas_call x1, Pallas kernels, in_one_kernel(): pl.pallas_call(functools.partial(fused, node_dev, rows, cols, side), out_...  91.5 us
    unnamed x6, local copies, waits for them, and re-layouts  6.23 us

profile of v3, /device:TPU:27, one launch (start us, length us, event | category | flops | bytes accessed | tf_op | source)
XLA Modules:
  0.0 100.5 jit_solution(13973392379085615986)
XLA Ops:
  1.3 0.7 convert_element_type.3
  2.0 0.0 copy-start
  2.0 0.8 copy.13.ids_col
  2.8 0.0 copy-done
  2.8 91.5 %shard_map.120 = (f32[256,256]{1,0:T(8,128)}, f32[256,256]{1,0:T(8,128)}, f32[256,256]{1,0:T(8,128)}, f32[1,256]{1,0:T(1,128)}) custom-call(f32[1,256]{1,0:T(1,128)} %bitcast.9, f32[256,1]{1,0:T(8,128)} %copy.13.ids_col, s32[1,256]{1,0:T(1,128)} %bitcast.10, s32[1,256]{1,0:T(1,128)} %bitcast.11, s32[1,1]{1,0:T(1,128)S(6)} %copy.18.live, f32[256,256]{1,0:T(8,128)} %feats.1, ...), custom_call_target="tpu_custom_call" | custom-call | tf_op jit(solution)/shard_map/pallas_call | solution.py:460
  94.3 1.7 %copy.19 = f32[256,256]{1,0:T(8,128)} copy(f32[256,256]{1,0:T(8,128)} %get-tuple-element.16) | data formatting | bytes 524288
  96.0 1.7 %copy.20 = f32[256,256]{1,0:T(8,128)} copy(f32[256,256]{1,0:T(8,128)} %get-tuple-element.17) | data formatting | bytes 524288
  97.7 1.7 %copy.21 = f32[256,256]{1,0:T(8,128)} copy(f32[256,256]{1,0:T(8,128)} %get-tuple-element.18) | data formatting | bytes 524288
  99.3 1.2 %copy.22 = f32[256]{0:T(256)} copy(f32[256]{0:T(256)} %bitcast.13) | data formatting | bytes 2048
Async XLA Ops:
  2.0 0.8 copy-start
